TPU v7x, 32 devices: a whole 2x2x4 slice. The times are simulated.
32 devices in a mesh: dp: 8 (over z, y), ctx: 4 (over x, core).
Axes of the slice: x: 2, y: 2, z: 4, core: 2. Of those that a mesh axis runs over, the one named last changes fastest.
Arguments:
- query_rows: bfloat16 [4096, 2048], P(('dp', 'ctx')), may hold values from -6 to 6
- key_rows: bfloat16 [4096, 2048], P(('dp', 'ctx')), may hold values from -6 to 6
- value_rows: bfloat16 [4096, 2048], P(('dp', 'ctx')), may hold values from -6 to 6
- target: bfloat16 [4096, 1536], P(('dp', 'ctx')), may hold values from -18 to 18
- w_out: bfloat16 [2048, 1536], replicated, may hold values from -0.125 to 0.125
- clip_lengths: int32 [8, 4], P('dp'), may hold values from 1 to 256, 512 in all within a row
- timesteps: int32 [8, 4], P('dp'), may hold values from 0 to 999
- tile_pattern: int32 [8, 4, 4], P('dp'), may hold values 0 or 1
- tau_prev: float32 [1], replicated, may hold values from 1 to 4
Outputs:
- query_grad: bfloat16 [4096, 2048], P(('dp', 'ctx'))
- key_grad: bfloat16 [4096, 2048], P(('dp', 'ctx'))
- value_grad: bfloat16 [4096, 2048], P(('dp', 'ctx'))
- weight_grad: float32 [2048, 1536], P('ctx', 'dp')
Inputs may be any that keep to these rules, and one draw needn't show every extreme that they name: `clip_lengths`: each row of clip lengths sums to 512, and its largest entry is 256.
All inputs are finite; a program needn't handle non-finite values. No bound on the sum of `tile_pattern` on one device may be relied on, other than what follows from the above.
Results may differ from a plain program's by a relative error of at most 0.019.
Values may be sent and summed in bfloat16 or wider, within the bound.
A program may use at most 128 MiB of HBM per device.

v0:
```python
import math

import jax
import jax.numpy as jnp
from jax import lax
from jax.sharding import PartitionSpec as P

HD = 128
OUT = 1536
CLIPS = 4
TILE = 128


MOMENTUM = 0.9


def clip_index(lengths_row, positions):
    ends = jnp.cumsum(lengths_row)
    return jnp.sum((positions[:, None] >= ends[None, :]).astype(jnp.int32), axis=1)


def attention_mask(clip_ids, pattern, row_total):
    tiles = row_total // TILE
    tile_ok = (
        jnp.broadcast_to(pattern[:, None, :, None], (tiles, TILE, tiles, TILE)).reshape(
            row_total, row_total
        )
        > 0
    )
    tile_ids = jnp.arange(row_total, dtype=jnp.int32) // TILE
    same_tile = tile_ids[:, None] == tile_ids[None, :]
    return (clip_ids[:, None] == clip_ids[None, :]) & (tile_ok | same_tile)


def head_probs(query_head, key_head, allowed):
    score_scale = 1.0 / math.sqrt(HD)
    scores = (
        lax.dot_general(
            query_head, key_head, (((1,), (1,)), ((), ())), preferred_element_type=jnp.float32
        )
        * score_scale
    )
    scores = jnp.where(allowed, scores, -1e30)
    row_max = jnp.max(scores, axis=1)
    unnorm = jnp.where(allowed, jnp.exp(scores - row_max[:, None]), 0.0)
    row_total = jnp.sum(unnorm, axis=1)
    return unnorm / row_total[:, None]


def head_backward(query_head, key_head, value_head, out_head, grad_head, allowed):
    score_scale = 1.0 / math.sqrt(HD)
    probs = head_probs(query_head, key_head, allowed)
    probs_low = probs.astype(jnp.bfloat16)
    value_grad = lax.dot_general(
        probs_low, grad_head, (((0,), (0,)), ((), ())), preferred_element_type=jnp.float32
    ).astype(jnp.bfloat16)
    prob_grad = lax.dot_general(
        grad_head, value_head, (((1,), (1,)), ((), ())), preferred_element_type=jnp.float32
    )
    delta = jnp.sum(grad_head.astype(jnp.float32) * out_head.astype(jnp.float32), axis=1)
    score_grad = (probs * (prob_grad - delta[:, None])).astype(jnp.bfloat16)
    query_grad = (
        jnp.dot(score_grad, key_head, preferred_element_type=jnp.float32) * score_scale
    ).astype(jnp.bfloat16)
    key_grad = (
        lax.dot_general(
            score_grad, query_head, (((0,), (0,)), ((), ())), preferred_element_type=jnp.float32
        )
        * score_scale
    ).astype(jnp.bfloat16)
    return (query_grad, key_grad, value_grad)


def superloss_weight(clip_loss, tau_now):
    argument = jnp.maximum(-0.3, 0.5 * (clip_loss - tau_now))
    branch = jnp.log1p(argument)
    for sweep in range(5):
        exp_value = jnp.exp(branch)
        branch = branch - (branch * exp_value - argument) / (exp_value * (branch + 1.0))
    return jnp.exp(-branch)


def on_device(
    query_rows, key_rows, value_rows, target, w_out, clip_lengths, timesteps, tile_pattern, tau_prev
):
    row_count = query_rows.shape[0]
    ctx_count = lax.axis_size("ctx")
    dp_count = lax.axis_size("dp")
    pack_rows = row_count * ctx_count
    ctx_place = lax.axis_index("ctx")
    query_head, key_head, value_head = (
        lax.all_to_all(query_rows, "ctx", split_axis=1, concat_axis=0, tiled=True),
        lax.all_to_all(key_rows, "ctx", split_axis=1, concat_axis=0, tiled=True),
        lax.all_to_all(value_rows, "ctx", split_axis=1, concat_axis=0, tiled=True),
    )
    lengths_row = clip_lengths[0]
    clip_pack = clip_index(lengths_row, jnp.arange(pack_rows, dtype=jnp.int32))
    allowed = attention_mask(clip_pack, tile_pattern[0], pack_rows)
    width_dev = query_head.shape[1]
    heads_dev = width_dev // HD
    head_outs = []
    for head in range(heads_dev):
        cols = slice(head * HD, (head + 1) * HD)
        probs = head_probs(query_head[:, cols], key_head[:, cols], allowed)
        head_outs.append(
            jnp.dot(
                probs.astype(jnp.bfloat16), value_head[:, cols], preferred_element_type=jnp.float32
            ).astype(jnp.bfloat16)
        )
    out_head = jnp.concatenate(head_outs, axis=1)
    out_rows = lax.all_to_all(out_head, "ctx", split_axis=0, concat_axis=1, tiled=True)
    predicted = jnp.dot(out_rows, w_out, preferred_element_type=jnp.float32)
    residue = predicted - target.astype(jnp.float32)
    row_squares = jnp.sum(residue * residue, axis=1)
    positions = ctx_place * row_count + jnp.arange(row_count, dtype=jnp.int32)
    clip_rows = clip_index(lengths_row, positions)
    onehot = (clip_rows[:, None] == jnp.arange(CLIPS, dtype=jnp.int32)[None, :]).astype(jnp.float32)
    partial_value = jnp.sum(row_squares[:, None] * onehot, axis=0)
    clip_len = lengths_row.astype(jnp.float32)
    step_weight = 1.0 + timesteps[0].astype(jnp.float32) / 250.0
    clip_sq = lax.psum(partial_value, "ctx")
    clip_loss = step_weight * clip_sq / (clip_len * OUT)
    loss_sum = lax.psum(jnp.sum(clip_loss), "dp")
    loss_mean = loss_sum / (dp_count * CLIPS)
    tau_now = MOMENTUM * tau_prev[0] + (1.0 - MOMENTUM) * loss_mean
    confidence = superloss_weight(clip_loss, tau_now)
    tokens_all = pack_rows * dp_count
    clip_scale = confidence * step_weight
    row_scale = jnp.sum(onehot * clip_scale[None, :], axis=1)
    pred_grad = (residue * row_scale[:, None]).astype(jnp.bfloat16)
    norm_factor = 1.0 / math.sqrt(tokens_all)
    pred_pack = lax.all_gather(pred_grad, "ctx", axis=0, tiled=True)
    w_block = lax.dynamic_slice_in_dim(w_out, ctx_place * width_dev, width_dev, 0)
    grad_head = lax.dot_general(
        pred_pack, w_block, (((1,), (1,)), ((), ())), preferred_element_type=jnp.float32
    ).astype(jnp.bfloat16)
    block_terms = (
        lax.dot_general(
            out_head, pred_pack, (((0,), (0,)), ((), ())), preferred_element_type=jnp.float32
        )
        * norm_factor
    )
    weight_grad = lax.psum_scatter(
        block_terms.astype(jnp.bfloat16), "dp", scatter_dimension=1, tiled=True
    ).astype(jnp.float32)
    parts_q, parts_k, parts_v = ([], [], [])
    for head in range(heads_dev):
        cols = slice(head * HD, (head + 1) * HD)
        grads = head_backward(
            query_head[:, cols],
            key_head[:, cols],
            value_head[:, cols],
            out_head[:, cols],
            grad_head[:, cols],
            allowed,
        )
        parts_q.append(grads[0])
        parts_k.append(grads[1])
        parts_v.append(grads[2])
    query_back, key_back, value_back = (
        lax.all_to_all(
            jnp.concatenate(parts_q, axis=1), "ctx", split_axis=0, concat_axis=1, tiled=True
        ),
        lax.all_to_all(
            jnp.concatenate(parts_k, axis=1), "ctx", split_axis=0, concat_axis=1, tiled=True
        ),
        lax.all_to_all(
            jnp.concatenate(parts_v, axis=1), "ctx", split_axis=0, concat_axis=1, tiled=True
        ),
    )
    return (query_back, key_back, value_back, weight_grad)


def solution(mesh):
    return jax.shard_map(
        on_device,
        mesh=mesh,
        in_specs=(
            P(("dp", "ctx"), None),
            P(("dp", "ctx"), None),
            P(("dp", "ctx"), None),
            P(("dp", "ctx"), None),
            P(),
            P("dp", None),
            P("dp", None),
            P("dp", None, None),
            P(),
        ),
        out_specs=(
            P(("dp", "ctx"), None),
            P(("dp", "ctx"), None),
            P(("dp", "ctx"), None),
            P("ctx", "dp"),
        ),
        check_vma=False,
    )
```

profile of v0, /device:TPU:8, one launch (start us, length us, event | category | flops | bytes accessed | tf_op | source)
XLA Modules:
  0.0 206.6 jit_solution(776329609303710735)
XLA Ops:
  7.2 2.1 %copy.64 = bf16[128,2048]{0,1:T(8,128)(2,1)} copy(bf16[128,2048]{1,0:T(8,128)(2,1)} %param.9) | data formatting | bytes 1048576 | tf_op args[0]
  9.3 3.6 %all-to-all-start = ((bf16[128,4,512]{0,2,1:T(8,128)(2,1)}), bf16[128,4,512]{0,2,1:T(8,128)(2,1)S(1)}, u32[]{:S(2)}, u32[]{:S(2)}) async-start(bf16[128,4,512]{0,2,1:T(8,128)(2,1)} %bitcast.3), calls=%async_computation | async-start | bytes 1048576 | tf_op jit(solution)/shard_map/all_to_all | solution.py:92
  13.9 7.8 %all-to-all-done = bf16[128,4,512]{0,2,1:T(8,128)(2,1)S(1)} async-done(((bf16[128,4,512]{0,2,1:T(8,128)(2,1)}), bf16[128,4,512]{0,2,1:T(8,128)(2,1)S(1)}, u32[]{:S(2)}, u32[]{:S(2)}) %all-to-all-start) | async-done | bytes 524320 | tf_op jit(solution)/shard_map/all_to_all | solution.py:92
  21.7 3.5 %all-to-all-start.1 = ((bf16[128,4,512]{0,2,1:T(8,128)(2,1)}), bf16[128,4,512]{0,2,1:T(8,128)(2,1)S(1)}, u32[]{:S(2)}, u32[]{:S(2)}) async-start(bf16[128,4,512]{0,2,1:T(8,128)(2,1)} %bitcast.6), calls=%async_computation.1 | async-start | bytes 1048576 | tf_op jit(solution)/shard_map/all_to_all | solution.py:93
  27.4 6.6 %all-to-all-done.1 = bf16[128,4,512]{0,2,1:T(8,128)(2,1)S(1)} async-done(((bf16[128,4,512]{0,2,1:T(8,128)(2,1)}), bf16[128,4,512]{0,2,1:T(8,128)(2,1)S(1)}, u32[]{:S(2)}, u32[]{:S(2)}) %all-to-all-start.1) | async-done | bytes 524320 | tf_op jit(solution)/shard_map/all_to_all | solution.py:93
  34.0 4.1 %all-to-all-start.2 = ((bf16[128,4,512]{0,2,1:T(8,128)(2,1)}), bf16[128,4,512]{0,2,1:T(8,128)(2,1)}, u32[]{:S(2)}, u32[]{:S(2)}) async-start(bf16[128,4,512]{0,2,1:T(8,128)(2,1)} %bitcast.9), calls=%async_computation.2 | async-start | bytes 1048576 | tf_op jit(solution)/shard_map/all_to_all | solution.py:94
  41.3 2.2 %fusion.108 = (f32[512]{0:T(512)S(1)}, f32[512,512]{0,1:T(8,128)}) fusion(pred[512,512]{0,1:T(32,128)(4,1)S(1)} %fusion.26, bf16[512,512]{1,0:T(8,128)(2,1)} %bitcast.90, bf16[512,512]{1,0:T(8,128)(2,1)S(1)} %bitcast.80), kind=kOutput, calls=%fused_computation.170 | convolution fusion | flops 67894784 | bytes 1574912 | tf_op jit(solution)/shard_map/dot_general | solution.py:38
  43.5 3.6 %all-to-all-done.2 = bf16[128,4,512]{0,2,1:T(8,128)(2,1)} async-done(((bf16[128,4,512]{0,2,1:T(8,128)(2,1)}), bf16[128,4,512]{0,2,1:T(8,128)(2,1)}, u32[]{:S(2)}, u32[]{:S(2)}) %all-to-all-start.2) | async-done | bytes 524320 | tf_op jit(solution)/shard_map/all_to_all | solution.py:94
  49.1 2.7 %fusion.28 = (f32[512]{0:T(512)S(1)}, f32[512]{0:T(512)S(1)}, f32[512]{0:T(512)S(1)}, f32[512]{0:T(512)S(1)}) fusion(f32[512,512]{0,1:T(8,128)} %get-tuple-element.23, f32[512]{0:T(512)S(1)} %get-tuple-element.22, f32[512,512]{0,1:T(8,128)S(1)} %get-tuple-element.25, f32[512]{0:T(512)S(1)} %get-tuple-element.24, f32[512,512]{0,1:T(8,128)S(1)} %get-tuple-element.27, ...), kind=kLoop, calls=%fused_computation.59 | loop fusion | flops 4192256 | bytes 4476928 | tf_op jit(solution)/shard_map/reduce_sum | solution.py:46
  55.5 3.5 %all-to-all-start.3 = ((bf16[4,128,512]{1,2,0:T(8,128)(2,1)}), bf16[4,128,512]{1,2,0:T(8,128)(2,1)S(1)}, u32[]{:S(2)}, u32[]{:S(2)}) async-start(bf16[4,128,512]{1,2,0:T(8,128)(2,1)} %copy_bitcast_fusion.3), calls=%async_computation.3 | async-start | bytes 1048576 | tf_op jit(solution)/shard_map/all_to_all | solution.py:111
  61.0 6.8 %all-to-all-done.3 = bf16[4,128,512]{1,2,0:T(8,128)(2,1)S(1)} async-done(((bf16[4,128,512]{1,2,0:T(8,128)(2,1)}), bf16[4,128,512]{1,2,0:T(8,128)(2,1)S(1)}, u32[]{:S(2)}, u32[]{:S(2)}) %all-to-all-start.3) | async-done | bytes 524320 | tf_op jit(solution)/shard_map/all_to_all | solution.py:111
  67.8 4.7 %multiply_reduce_fusion = (f32[128]{0:T(128)S(1)}, f32[128,1536]{1,0:T(8,128)}) fusion(bf16[128,1536]{1,0:T(8,128)(2,1)} %param.12, bf16[128,2048]{0,1:T(8,128)(2,1)S(1)} %bitcast.95, bf16[2048,1536]{1,0:T(8,128)(2,1)} %param.13), kind=kOutput, calls=%fused_computation.57 | convolution fusion | flops 806092672 | bytes 7995904 | tf_op jit(solution)/shard_map/dot_general | solution.py:112
  72.6 5.8 %psum.14 = f32[4]{0:T(128)S(1)} all-reduce(f32[4]{0:T(128)S(1)} %select_reduce_fusion.1), channel_id=1, replica_groups=mesh['dp'=8,'ctx'=4] {'ctx'}, use_global_device_ids=true, to_apply=%region_13.14 | all-reduce | flops 4 | bytes 32 | tf_op jit(solution)/shard_map/psum | solution.py:121
  79.7 19.5 %psum.15 = f32[]{:T(128)} all-reduce(f32[]{:T(128)} %get-tuple-element.20), channel_id=1, replica_groups=mesh['dp'=8,'ctx'=4] {'dp'}, use_global_device_ids=true, to_apply=%region_15.16 | all-reduce | flops 1 | bytes 8 | tf_op jit(solution)/shard_map/psum | solution.py:123
  103.4 19.4 %all-gather.2.cloned.1.call-done = bf16[512,1536]{1,0:T(8,128)(2,1)} async-done(((bf16[128,1536]{1,0:T(8,128)(2,1)}), bf16[512,1536]{1,0:T(8,128)(2,1)}) %all-gather.2.cloned.1.call-update) | async-done | bytes 1572880 | tf_op jit(solution)/shard_map/all_gather | solution.py:132
  122.8 3.0 %fusion.15 = bf16[512,512]{0,1:T(8,128)(2,1)S(1)} fusion(bf16[512,1536]{1,0:T(8,128)(2,1)} %all-gather.2.cloned.1.call-done, bf16[2048,1536]{1,0:T(8,128)(2,1)} %param.13, s32[]{:T(128)S(6)} %select_n.58), kind=kOutput, calls=%fused_computation.25 | convolution fusion | flops 805568512 | bytes 3670020 | tf_op jit(solution)/shard_map/dot_general | solution.py:134
  131.2 2.2 %fusion = bf16[512,1536]{0,1:T(8,128)(2,1)} fusion(bf16[512,1536]{1,0:T(8,128)(2,1)S(1)} %copy-done.43, bf16[512,128]{0,1:T(8,128)(2,1)S(1)} %copy-done.18, bf16[512,128]{0,1:T(8,128)(2,1)S(1)} %copy-done.16, bf16[512,128]{0,1:T(8,128)(2,1)S(1)} %convolution_convert_fusion.6, bf16[512,128]{0,1:T(8,128)(2,1)S(1)} %copy-done.20), kind=kOutput, calls=%fused_computation.1 | convolution fusion | flops 808976384 | bytes 3670016 | tf_op jit(solution)/shard_map/dot_general | solution.py:138
  135.3 4.3 %all-to-all-start.6 = ((bf16[4,128,512]{1,2,0:T(8,128)(2,1)}), bf16[4,128,512]{1,2,0:T(8,128)(2,1)}, u32[]{:S(2)}, u32[]{:S(2)}) async-start(bf16[4,128,512]{1,2,0:T(8,128)(2,1)} %copy_bitcast_fusion), calls=%async_computation.6 | async-start | bytes 1048576 | tf_op jit(solution)/shard_map/all_to_all | solution.py:167
  148.4 3.5 %all-to-all-start.5 = ((bf16[4,128,512]{1,2,0:T(8,128)(2,1)}), bf16[4,128,512]{1,2,0:T(8,128)(2,1)S(1)}, u32[]{:S(2)}, u32[]{:S(2)}) async-start(bf16[4,128,512]{1,2,0:T(8,128)(2,1)} %copy_bitcast_fusion.1), calls=%async_computation.5 | async-start | bytes 1048576 | tf_op jit(solution)/shard_map/all_to_all | solution.py:164
  153.3 7.4 %all-to-all-done.5 = bf16[4,128,512]{1,2,0:T(8,128)(2,1)S(1)} async-done(((bf16[4,128,512]{1,2,0:T(8,128)(2,1)}), bf16[4,128,512]{1,2,0:T(8,128)(2,1)S(1)}, u32[]{:S(2)}, u32[]{:S(2)}) %all-to-all-start.5) | async-done | bytes 524320 | tf_op jit(solution)/shard_map/all_to_all | solution.py:164
  160.7 3.5 %all-to-all-start.4 = ((bf16[4,128,512]{1,2,0:T(8,128)(2,1)}), bf16[4,128,512]{1,2,0:T(8,128)(2,1)S(1)}, u32[]{:S(2)}, u32[]{:S(2)}) async-start(bf16[4,128,512]{1,2,0:T(8,128)(2,1)} %copy_bitcast_fusion.2), calls=%async_computation.4 | async-start | bytes 1048576 | tf_op jit(solution)/shard_map/all_to_all | solution.py:161
  164.2 2.0 copy.80
  167.2 5.8 %all-to-all-done.4 = bf16[4,128,512]{1,2,0:T(8,128)(2,1)S(1)} async-done(((bf16[4,128,512]{1,2,0:T(8,128)(2,1)}), bf16[4,128,512]{1,2,0:T(8,128)(2,1)S(1)}, u32[]{:S(2)}, u32[]{:S(2)}) %all-to-all-start.4) | async-done | bytes 524320 | tf_op jit(solution)/shard_map/all_to_all | solution.py:161
  174.0 24.1 %reduce-scatter.2.cloned.1.call-done = bf16[512,192]{0,1:T(8,128)(2,1)} async-done(((bf16[512,1536]{0,1:T(8,128)(2,1)}), bf16[512,192]{0,1:T(8,128)(2,1)}) %reduce-scatter.2.cloned.1.call-update) | async-done | bytes 196624 | tf_op jit(solution)/shard_map/reduce_scatter | solution.py:143
  (145 shorter events, 39.2 us)
Async XLA Ops:
  7.2 5.7 %copy-start.9 = (bf16[128,2048]{1,0:T(8,128)(2,1)S(1)}, bf16[128,2048]{1,0:T(8,128)(2,1)}, u32[]{:S(2)}) copy-start(bf16[128,2048]{1,0:T(8,128)(2,1)} %param.10) | copy-start | bytes 1572868
  7.2 6.7 %copy-start.40 = (s32[1,4,4]{2,1,0:T(4,128)S(1)}, s32[1,4,4]{2,1,0:T(4,128)}, u32[]{:S(2)}) copy-start(s32[1,4,4]{2,1,0:T(4,128)} %param.16) | copy-start | bytes 196
  9.3 16.0 %copy-start.10 = (bf16[128,2048]{1,0:T(8,128)(2,1)S(1)}, bf16[128,2048]{1,0:T(8,128)(2,1)}, u32[]{:S(2)}) copy-start(bf16[128,2048]{1,0:T(8,128)(2,1)} %param.11) | copy-start | bytes 1572868
  9.3 12.4 %all-to-all-start = ((bf16[128,4,512]{0,2,1:T(8,128)(2,1)}), bf16[128,4,512]{0,2,1:T(8,128)(2,1)S(1)}, u32[]{:S(2)}, u32[]{:S(2)}) async-start(bf16[128,4,512]{0,2,1:T(8,128)(2,1)} %bitcast.3), calls=%async_computation | async-start | bytes 1048576 | tf_op jit(solution)/shard_map/all_to_all | solution.py:92
  12.9 13.4 %copy-start.41 = (s32[1,4]{1,0:T(1,128)S(1)}, s32[1,4]{1,0:T(1,128)}, u32[]{:S(2)}) copy-start(s32[1,4]{1,0:T(1,128)} %param.14) | copy-start | bytes 52
  21.7 12.3 %all-to-all-start.1 = ((bf16[128,4,512]{0,2,1:T(8,128)(2,1)}), bf16[128,4,512]{0,2,1:T(8,128)(2,1)S(1)}, u32[]{:S(2)}, u32[]{:S(2)}) async-start(bf16[128,4,512]{0,2,1:T(8,128)(2,1)} %bitcast.6), calls=%async_computation.1 | async-start | bytes 1048576 | tf_op jit(solution)/shard_map/all_to_all | solution.py:93
  34.0 13.1 %all-to-all-start.2 = ((bf16[128,4,512]{0,2,1:T(8,128)(2,1)}), bf16[128,4,512]{0,2,1:T(8,128)(2,1)}, u32[]{:S(2)}, u32[]{:S(2)}) async-start(bf16[128,4,512]{0,2,1:T(8,128)(2,1)} %bitcast.9), calls=%async_computation.2 | async-start | bytes 1048576 | tf_op jit(solution)/shard_map/all_to_all | solution.py:94
  49.1 2.7 %copy-start.2 = (f32[512,512]{0,1:T(8,128)S(1)}, f32[512,512]{0,1:T(8,128)}, u32[]{:S(2)}) copy-start(f32[512,512]{0,1:T(8,128)} %get-tuple-element.29) | copy-start | bytes 3145732
  49.1 2.7 %copy-start.11 = (bf16[4,128,512]{2,1,0:T(8,128)(2,1)S(1)}, bf16[4,128,512]{2,1,0:T(8,128)(2,1)}, u32[]{:S(2)}) copy-start(bf16[4,128,512]{2,1,0:T(8,128)(2,1)} %copy.69) | copy-start | bytes 1572868
  55.5 12.3 %all-to-all-start.3 = ((bf16[4,128,512]{1,2,0:T(8,128)(2,1)}), bf16[4,128,512]{1,2,0:T(8,128)(2,1)S(1)}, u32[]{:S(2)}, u32[]{:S(2)}) async-start(bf16[4,128,512]{1,2,0:T(8,128)(2,1)} %copy_bitcast_fusion.3), calls=%async_computation.3 | async-start | bytes 1048576 | tf_op jit(solution)/shard_map/all_to_all | solution.py:111
  59.0 63.8 %all-gather.2.cloned.1.call-start = ((), (), s32[]{:S(2)}) async-start(), calls=%async_computation.8 | async-start | bytes 1966080 | tf_op jit(solution)/shard_map/all_gather | solution.py:132
  67.8 4.7 %copy-start.44 = (s32[128]{0:T(128)S(1)}, s32[128]{0:T(128)}, u32[]{:S(2)}) copy-start(s32[128]{0:T(128)} %convert_reduce_fusion.1) | copy-start | bytes 1540
  103.3 94.7 %reduce-scatter.2.cloned.1.call-start = ((), (), s32[]{:S(2)}) async-start(), calls=%async_computation.9 | async-start | bytes 1769472 | tf_op jit(solution)/shard_map/reduce_scatter | solution.py:143
  103.4 22.4 %copy-start.34 = (f32[512]{0:T(512)S(1)}, f32[512]{0:T(512)}, u32[]{:S(2)}) copy-start(f32[512]{0:T(512)} %copy-done.33) | copy-start | bytes 6148
  122.8 3.0 %copy-start.1 = (f32[512,512]{0,1:T(8,128)S(1)}, f32[512,512]{0,1:T(8,128)}, u32[]{:S(2)}) copy-start(f32[512,512]{0,1:T(8,128)} %get-tuple-element.23) | copy-start | bytes 3145732
  125.8 4.7 %copy-start.13 = (bf16[512,512]{0,1:T(8,128)(2,1)}, bf16[512,512]{0,1:T(8,128)(2,1)S(1)}, u32[]{:S(2)}) copy-start(bf16[512,512]{0,1:T(8,128)(2,1)S(1)} %fusion.15) | copy-start | bytes 1572868
  133.4 6.2 %copy-start.35 = (f32[512]{0:T(512)S(1)}, f32[512]{0:T(512)}, u32[]{:S(2)}) copy-start(f32[512]{0:T(512)} %copy-done.33) | copy-start | bytes 6148
  133.4 6.2 %copy-start.39 = (f32[512]{0:T(512)S(1)}, f32[512]{0:T(512)}, u32[]{:S(2)}) copy-start(f32[512]{0:T(512)} %get-tuple-element.12) | copy-start | bytes 6148
  135.3 13.0 %all-to-all-start.6 = ((bf16[4,128,512]{1,2,0:T(8,128)(2,1)}), bf16[4,128,512]{1,2,0:T(8,128)(2,1)}, u32[]{:S(2)}, u32[]{:S(2)}) async-start(bf16[4,128,512]{1,2,0:T(8,128)(2,1)} %copy_bitcast_fusion), calls=%async_computation.6 | async-start | bytes 1048576 | tf_op jit(solution)/shard_map/all_to_all | solution.py:167
  139.7 2.3 %copy-start.6 = (bf16[4,128,512]{2,1,0:T(8,128)(2,1)S(1)}, bf16[4,128,512]{2,1,0:T(8,128)(2,1)}, u32[]{:S(2)}) copy-start(bf16[4,128,512]{2,1,0:T(8,128)(2,1)} %copy-done.5) | copy-start | bytes 1572868
  139.7 2.6 %copy-start.14 = (bf16[512,512]{0,1:T(8,128)(2,1)S(1)}, bf16[512,512]{0,1:T(8,128)(2,1)}, u32[]{:S(2)}) copy-start(bf16[512,512]{0,1:T(8,128)(2,1)} %copy-done.13) | copy-start | bytes 1572868
  145.3 6.6 %copy-start.8 = (bf16[512,512]{0,1:T(8,128)(2,1)S(1)}, bf16[512,512]{0,1:T(8,128)(2,1)}, u32[]{:S(2)}) copy-start(bf16[512,512]{0,1:T(8,128)(2,1)} %copy-done.7) | copy-start | bytes 1572868
  148.4 12.3 %all-to-all-start.5 = ((bf16[4,128,512]{1,2,0:T(8,128)(2,1)}), bf16[4,128,512]{1,2,0:T(8,128)(2,1)S(1)}, u32[]{:S(2)}, u32[]{:S(2)}) async-start(bf16[4,128,512]{1,2,0:T(8,128)(2,1)} %copy_bitcast_fusion.1), calls=%async_computation.5 | async-start | bytes 1048576 | tf_op jit(solution)/shard_map/all_to_all | solution.py:164
  160.7 12.3 %all-to-all-start.4 = ((bf16[4,128,512]{1,2,0:T(8,128)(2,1)}), bf16[4,128,512]{1,2,0:T(8,128)(2,1)S(1)}, u32[]{:S(2)}, u32[]{:S(2)}) async-start(bf16[4,128,512]{1,2,0:T(8,128)(2,1)} %copy_bitcast_fusion.2), calls=%async_computation.4 | async-start | bytes 1048576 | tf_op jit(solution)/shard_map/all_to_all | solution.py:161
  (30 other events, 33.1 us)
Sparse Core Ops, SparseCore 0:
  103.5 19.2 all-gather.1
  133.6 64.4 reduce-scatter.1
where the time goes:
time: 210 us; the launch traced here: 207 us
  waiting for transfers between devices  83.3 us (40%)
  starting transfers between devices  26 us (12%)
  matrix products  25.8 us (12%)
  blocking collectives  25.3 us (12%)
  between operations  16 us (8%)
  other arithmetic  15.5 us (7%)
  local copies, waits for them, and re-layouts  14.7 us (7%)
    reduce_scatter x1, waiting for transfers between devices, on_device(): lax.psum_scatter(block_terms.astype(jnp.bfloat16), 'dp', scatter_dimensio...  24.1 us
    psum x1, blocking collectives, on_device(): loss_sum = lax.psum(jnp.sum(clip_loss), 'dp')  19.5 us
    all_gather x1, waiting for transfers between devices, on_device(): pred_pack = lax.all_gather(pred_grad, 'ctx', axis=0, tiled=True)  19.4 us
    unnamed x96, local copies, waits for them, and re-layouts  11.9 us
    all_to_all x1, waiting for transfers between devices, on_device(): lax.all_to_all(query_rows, 'ctx', split_axis=1, concat_axis=0, tiled=True)  7.78 us
    all_to_all x1, waiting for transfers between devices, on_device(): lax.all_to_all(jnp.concatenate(parts_k, axis=1), 'ctx', split_axis=0, con...  7.37 us
    all_to_all x1, waiting for transfers between devices, on_device(): lax.all_to_all(out_head, 'ctx', split_axis=0, concat_axis=1, tiled=True)  6.79 us
    all_to_all x1, waiting for transfers between devices, on_device(): lax.all_to_all(key_rows, 'ctx', split_axis=1, concat_axis=0, tiled=True)  6.59 us
  transfers between devices with their start and end apart: 9, of which 9 were waited for; matrix products, arithmetic and copies ran while one was open for 11% of the time, Pallas kernels for 0%

commit v1 on v0

v1 whole, which is shorter than its diff:
```python
import functools
import math

import jax
import jax.numpy as jnp
from jax import lax
from jax.experimental import pallas as pl
from jax.experimental.pallas import tpu as pltpu
from jax.sharding import PartitionSpec as P

HD = 128
OUT = 1536
CLIPS = 4
TILE = 128
MOMENTUM = 0.9
F32 = jnp.float32
BF16 = jnp.bfloat16
CHUNK = 512


def dot_nt(a, b):
    return lax.dot_general(a, b, (((1,), (1,)), ((), ())), preferred_element_type=F32)


def dot_nn(a, b):
    return jnp.dot(a, b, preferred_element_type=F32)


def dot_tn(a, b):
    return lax.dot_general(a, b, (((0,), (0,)), ((), ())), preferred_element_type=F32)


def superloss_weight(clip_loss, tau_now):
    argument = jnp.maximum(-0.3, 0.5 * (clip_loss - tau_now))
    branch = jnp.log1p(argument)
    for sweep in range(5):
        exp_value = jnp.exp(branch)
        branch = branch - (branch * exp_value - argument) / (exp_value * (branch + 1.0))
    return jnp.exp(-branch)


def kernel(
    C, NY, NZ, RB, DA,
    q_in, k_in, v_in, tgt_in, w_in, len_s, time_s, pat_s, tau_s,
    qg, kg, vg, wg,
    qh, kh, vh, bias, probs, oh, osc, orow, w_v, tgt_v, respack, graw, gh,
    dqh, dkh, dvh, wt, yrecv, zsend, zrecv, wacc, lsend, lctx, ly, lz,
    local_sem, in_send, in_recv, out_send, out_recv, lc_send, lc_recv, ly_send, ly_recv,
    lz_send, lz_recv, res_send, res_recv, rel_send, rel_recv, wy_send, wy_recv, wz_send, wz_recv,
    gr_send, gr_recv, own_sem,
):
    PR = RB * C
    WD = DA // C
    H = WD // HD
    X = C // 2
    DP = NY * NZ
    B = OUT // DP
    NT = PR // TILE
    NCH = OUT // CHUNK
    me = lax.axis_index("ctx")
    dp = lax.axis_index("dp")
    xi, core = me // 2, lax.rem(me, 2)
    zi, yi = dp // NY, lax.rem(dp, NY)
    sib = xi * 2 + (1 - core)

    def ctx_peer(o):
        return lax.rem(me + o, C)

    def ctx_src(o):
        return lax.rem(me + C - o, C)

    def x_peer(o):
        return lax.rem(xi + o, X) * 2 + core

    def y_dev(o):
        return zi * NY + lax.rem(yi + o, NY)

    def z_dev(k):
        return lax.rem(zi + k, NZ) * NY + yi

    def rows(p, n=RB):
        return pl.ds(pl.multiple_of(p * n, n), n)

    def cols(base, h):
        return pl.ds(pl.multiple_of(base + h * HD, HD), HD)

    def remote(src, dst, ss, rs, where):
        return pltpu.make_async_remote_copy(
            src_ref=src, dst_ref=dst, send_sem=ss, recv_sem=rs,
            device_id=where, device_id_type=pl.DeviceIdType.MESH,
        )

    ins, heads_in = (q_in, k_in, v_in), (qh, kh, vh)
    grads_h, grads_out = (dqh, dkh, dvh), (qg, kg, vg)

    def local_in(t):
        return pltpu.make_async_copy(
            ins[t].at[:, pl.ds(pl.multiple_of(me * WD, WD), WD)], heads_in[t].at[rows(me), :],
            local_sem.at[t])

    copy_t = pltpu.make_async_copy(tgt_in, tgt_v, local_sem.at[3])
    copy_w = pltpu.make_async_copy(w_in, w_v, local_sem.at[4])
    for t in range(3):
        local_in(t).start()
    copy_t.start()
    copy_w.start()

    barrier = pltpu.get_barrier_semaphore()
    for o in range(1, C):
        pl.semaphore_signal(barrier, inc=1, device_id={"ctx": ctx_peer(o)},
                            device_id_type=pl.DeviceIdType.MESH)
    for o in range(1, NY):
        pl.semaphore_signal(barrier, inc=1, device_id={"dp": y_dev(o)},
                            device_id_type=pl.DeviceIdType.MESH)
    for k in range(1, NZ):
        pl.semaphore_signal(barrier, inc=1, device_id={"dp": z_dev(k)},
                            device_id_type=pl.DeviceIdType.MESH)
    pl.semaphore_wait(barrier, (C - 1) + (NY - 1) + (NZ - 1))

    def in_copy(t, h, o):
        p = ctx_peer(o)
        return remote(ins[t].at[:, cols(p * WD, h)], heads_in[t].at[rows(me), cols(0, h)],
                      in_send.at[t, h, o], in_recv.at[t, h, o], {"ctx": p})

    @pl.loop(0, H)
    def _(h):
        for o in range(1, C):
            for t in range(3):
                in_copy(t, h, o).start()

    ends = []
    for c in range(CLIPS):
        ends.append(len_s[0, c] if c == 0 else ends[-1] + len_s[0, c])

    def clip_of(pos):
        total = (pos >= ends[0]).astype(jnp.int32)
        for c in range(1, CLIPS):
            total = total + (pos >= ends[c]).astype(jnp.int32)
        return total

    @pl.loop(0, NT)
    def _(i):
        rpos = lax.broadcasted_iota(jnp.int32, (TILE, PR), 0) + i * TILE
        cpos = lax.broadcasted_iota(jnp.int32, (TILE, PR), 1)
        tile = cpos // TILE
        ok = (tile == i).astype(jnp.int32)
        for j in range(NT):
            ok = jnp.where(tile == j, jnp.maximum(ok, pat_s[0, i, j]), ok)
        allowed = (clip_of(rpos) == clip_of(cpos)) & (ok > 0)
        bias[rows(i, TILE), :] = jnp.where(allowed, 0.0, -1e30)

    scale = 1.0 / math.sqrt(HD)
    for t in range(3):
        local_in(t).wait()

    def out_copy(h, o):
        p = ctx_peer(o)
        return remote(oh.at[rows(p), cols(0, h)], orow.at[:, cols(me * WD, h)],
                      out_send.at[h, o], out_recv.at[h, o], {"ctx": p})

    @pl.loop(0, H)
    def _(h):
        for o in range(1, C):
            for t in range(3):
                in_copy(t, h, o).wait_recv()
        k = kh[:, cols(0, h)]
        v = vh[:, cols(0, h)]
        for i in range(NT):
            rr = slice(i * TILE, (i + 1) * TILE)
            s = dot_nt(qh[rr, cols(0, h)], k) * scale + bias[rr, :]
            e = jnp.exp(s - jnp.max(s, axis=1, keepdims=True))
            p = e * (1.0 / jnp.sum(e, axis=1, keepdims=True))
            probs[h, rr, :] = p
            oh[rr, cols(0, h)] = dot_nn(p.astype(BF16), v).astype(BF16)
        for o in range(1, C):
            out_copy(h, o).start()
        orow[:, cols(me * WD, h)] = oh[rows(me), cols(0, h)]

    copy_t.wait()
    copy_w.wait()

    @pl.loop(0, H)
    def _(h):
        for o in range(1, C):
            out_copy(h, o).wait_recv()

    rowsq = jnp.zeros((RB, 1), F32)
    for n in range(NCH):
        cc = slice(n * CHUNK, (n + 1) * CHUNK)
        res = dot_nn(orow[...], w_v[:, cc]) - tgt_v[:, cc].astype(F32)
        rowsq = rowsq + jnp.sum(res * res, axis=1, keepdims=True)
        respack[rows(me), cc] = res.astype(BF16)

    lane = lax.broadcasted_iota(jnp.int32, (RB, 128), 1)
    own_clip = clip_of(lax.broadcasted_iota(jnp.int32, (RB, 128), 0) + me * RB)
    part = jnp.sum(jnp.where(own_clip == lane, rowsq, 0.0), axis=0, keepdims=True)
    lsend[0] = jnp.broadcast_to(part, (8, 128))

    def lctx_copy(o):
        return remote(lsend.at[0], lctx.at[o], lc_send.at[o], lc_recv.at[o], {"ctx": ctx_peer(o)})

    def ly_copy(o):
        return remote(lsend.at[1], ly.at[o], ly_send.at[o], ly_recv.at[o], {"dp": y_dev(o)})

    def lz_copy(k):
        return remote(lsend.at[2], lz.at[k], lz_send.at[k], lz_recv.at[k], {"dp": z_dev(k)})

    for o in range(1, C):
        lctx_copy(o).start()

    def res_view(p, n):
        return respack.at[rows(p), pl.ds(n * CHUNK, CHUNK)]

    def res_copy(n, o):
        p = sib if o == 0 else x_peer(o)
        return remote(res_view(me, n), res_view(me, n), res_send.at[n, o], res_recv.at[n, o],
                      {"ctx": p})

    def relay_copy(n, o):
        p = lax.rem(xi + X - o, X) * 2 + core
        return remote(res_view(p, n), res_view(p, n), rel_send.at[n, o], rel_recv.at[n, o],
                      {"ctx": sib})

    for n in range(NCH):
        for o in range(1, X):
            res_copy(n, o).start()
    for n in range(NCH):
        res_copy(n, 0).start()

    def grad_rows(p):
        graw[rows(p), :] = dot_nt(respack[rows(p), :], w_v[rows(me, WD), :])

    grad_rows(me)
    lanes8 = lax.broadcasted_iota(jnp.int32, (8, 128), 1)
    length = jnp.ones((8, 128), F32)
    weight = jnp.zeros((8, 128), F32)
    for c in range(CLIPS):
        length = jnp.where(lanes8 == c, len_s[0, c].astype(F32), length)
        weight = jnp.where(lanes8 == c, 1.0 + time_s[0, c].astype(F32) / 250.0, weight)
    clip_sq = lsend[0]
    for o in range(1, C):
        lctx_copy(o).wait_recv()
        clip_sq = clip_sq + lctx[o]
    clip_loss = weight * clip_sq / (length * OUT)
    loss_sum = jnp.broadcast_to(jnp.sum(clip_loss, axis=1, keepdims=True), (8, 128))
    lsend[1] = loss_sum
    for o in range(1, NY):
        ly_copy(o).start()

    for n in range(NCH):
        res_copy(n, 0).wait_recv()
    grad_rows(sib)
    for o in range(1, NY):
        ly_copy(o).wait_recv()
        loss_sum = loss_sum + ly[o]
    lsend[2] = loss_sum
    for k in range(1, NZ):
        lz_copy(k).start()

    for n in range(NCH):
        for o in range(1, X):
            res_copy(n, o).wait_recv()
            relay_copy(n, o).start()
    for o in range(1, X):
        grad_rows(lax.rem(xi + X - o, X) * 2 + core)

    for k in range(1, NZ):
        lz_copy(k).wait_recv()
        loss_sum = loss_sum + lz[k]
    tau_now = MOMENTUM * tau_s[0] + (1.0 - MOMENTUM) * (loss_sum / (DP * CLIPS))
    clip_scale = (superloss_weight(clip_loss, tau_now) * weight)[0:1, :]
    norm = 1.0 / math.sqrt(PR * DP)

    def row_scale(i):
        pos = lax.broadcasted_iota(jnp.int32, (RB, 128), 0) + i * RB
        return jnp.sum(jnp.where(clip_of(pos) == lane, clip_scale, 0.0), axis=1, keepdims=True)

    scales = [row_scale(i) for i in range(C)]
    for i in range(C):
        rr = slice(i * RB, (i + 1) * RB)
        osc[rr, :] = (oh[rr, :].astype(F32) * (scales[i] * norm)).astype(BF16)

    for n in range(NCH):
        for o in range(1, X):
            relay_copy(n, o).wait_recv()
    for o in range(1, X):
        grad_rows(lax.rem(xi + X - o, X) * 2 + (1 - core))
    for i in range(C):
        rr = slice(i * RB, (i + 1) * RB)
        gh[rr, :] = (graw[rr, :] * scales[i]).astype(BF16)

    @pl.loop(0, OUT // 256)
    def _(n):
        wt[rows(n, 256), :] = dot_tn(respack[:, rows(n, 256)], osc[...]).astype(BF16)

    def wy_copy(o, k):
        kk = lax.rem(zi + k, NZ)
        return remote(wt.at[rows(kk * NY + lax.rem(yi + o, NY), B), :], yrecv.at[o, lax.rem(k, NZ)],
                      wy_send.at[o, lax.rem(k, NZ)], wy_recv.at[o, lax.rem(k, NZ)],
                      {"dp": y_dev(o)})

    def wz_copy(k):
        return remote(zsend.at[k], zrecv.at[k], wz_send.at[k], wz_recv.at[k], {"dp": z_dev(k)})

    def y_total(k):
        total = wt[rows(lax.rem(zi + k, NZ) * NY + yi, B), :].astype(F32)
        for o in range(1, NY):
            wy_copy(o, k).wait_recv()
            total = total + yrecv[o, lax.rem(k, NZ)].astype(F32)
        return total

    @pl.loop(1, NZ + 1)
    def _(k):
        for o in range(1, NY):
            wy_copy(o, k).start()

    def grad_copy(t, h, o):
        p = ctx_peer(o)
        return remote(grads_h[t].at[rows(p), cols(0, h)], grads_out[t].at[:, cols(me * WD, h)],
                      gr_send.at[t, h, o], gr_recv.at[t, h, o], {"ctx": p})

    def own_grad(t):
        return pltpu.make_async_copy(
            grads_h[t].at[rows(me), :],
            grads_out[t].at[:, pl.ds(pl.multiple_of(me * WD, WD), WD)], own_sem.at[t])

    per_head = -(-NZ // H)

    @pl.loop(0, H)
    def _(h):
        hc = cols(0, h)
        k = kh[:, hc]
        v = vh[:, hc]
        dk_t = jnp.zeros((HD, PR), F32)
        dv_t = jnp.zeros((HD, PR), F32)
        for i in range(NT):
            rr = slice(i * TILE, (i + 1) * TILE)
            g = gh[rr, hc]
            p = probs[h, rr, :]
            gf = g.astype(F32)
            delta = jnp.sum(gf * oh[rr, hc].astype(F32), axis=1, keepdims=True)
            ds = (p * (dot_nt(g, v) - delta)).astype(BF16)
            dqh[rr, hc] = (dot_nn(ds, k) * scale).astype(BF16)
            dk_t = dk_t + dot_nn(qh[rr, hc].T, ds)
            dv_t = dv_t + dot_nn(g.T, p.astype(BF16))
        dkh[:, hc] = (dk_t * scale).T.astype(BF16)
        dvh[:, hc] = dv_t.T.astype(BF16)
        for o in range(1, C):
            for t in range(3):
                grad_copy(t, h, o).start()
        for kk in range(per_head):
            step = h * per_head + kk + 1

            @pl.when(step < NZ)
            def _():
                zsend[step] = y_total(step).astype(BF16)
                wz_copy(step).start()

    for t in range(3):
        own_grad(t).start()
    wacc[...] = y_total(NZ)
    total = wacc[...]
    for k in range(1, NZ):
        wz_copy(k).wait_recv()
        total = total + zrecv[k].astype(F32)
    wg[...] = total.T

    @pl.loop(0, H)
    def _(h):
        for o in range(1, C):
            out_copy(h, o).wait_send()
            for t in range(3):
                in_copy(t, h, o).wait_send()
                grad_copy(t, h, o).wait_send()
                grad_copy(t, h, o).wait_recv()

    for o in range(1, C):
        lctx_copy(o).wait_send()
    for o in range(1, NY):
        ly_copy(o).wait_send()
    for k in range(1, NZ):
        lz_copy(k).wait_send()
        wz_copy(k).wait_send()
    for n in range(NCH):
        for o in range(X):
            res_copy(n, o).wait_send()
        for o in range(1, X):
            relay_copy(n, o).wait_send()

    @pl.loop(1, NZ + 1)
    def _(k):
        for o in range(1, NY):
            wy_copy(o, k).wait_send()

    for t in range(3):
        own_grad(t).wait()


def on_device(
    query_rows, key_rows, value_rows, target, w_out, clip_lengths, timesteps, tile_pattern, tau_prev
):
    RB, DA = query_rows.shape
    C = lax.axis_size("ctx")
    DP = lax.axis_size("dp")
    NY = 2 ** ((DP.bit_length() - 1) // 2)
    NZ = DP // NY
    PR, WD, B = RB * C, DA // C, OUT // DP
    H, X, NCH = WD // HD, C // 2, OUT // CHUNK
    dma = pltpu.SemaphoreType.DMA
    vm = pltpu.VMEM
    anyspec = pl.BlockSpec(memory_space=pl.ANY)
    smem = pl.BlockSpec(memory_space=pltpu.SMEM)
    rows_shape = jax.ShapeDtypeStruct((RB, DA), BF16)
    scratch = [
        vm((PR, WD), BF16), vm((PR, WD), BF16), vm((PR, WD), BF16),
        vm((PR, PR), F32), vm((H, PR, PR), F32), vm((PR, WD), BF16), vm((PR, WD), BF16),
        vm((RB, DA), BF16), vm((DA, OUT), BF16), vm((RB, OUT), BF16), vm((PR, OUT), BF16),
        vm((PR, WD), F32), vm((PR, WD), BF16),
        vm((PR, WD), BF16), vm((PR, WD), BF16), vm((PR, WD), BF16),
        vm((OUT, WD), BF16), vm((NY, NZ, B, WD), BF16), vm((NZ, B, WD), BF16),
        vm((NZ, B, WD), BF16), vm((B, WD), F32),
        vm((3, 8, 128), F32), vm((C, 8, 128), F32), vm((NY, 8, 128), F32), vm((NZ, 8, 128), F32),
        dma((5,)), dma((3, H, C)), dma((3, H, C)), dma((H, C)), dma((H, C)),
        dma((C,)), dma((C,)), dma((NY,)), dma((NY,)), dma((NZ,)), dma((NZ,)),
        dma((NCH, X)), dma((NCH, X)), dma((NCH, X)), dma((NCH, X)),
        dma((NY, NZ)), dma((NY, NZ)), dma((NZ,)), dma((NZ,)),
        dma((3, H, C)), dma((3, H, C)), dma((3,)),
    ]
    return pl.pallas_call(
        functools.partial(kernel, C, NY, NZ, RB, DA),
        out_shape=(rows_shape, rows_shape, rows_shape, jax.ShapeDtypeStruct((WD, B), F32)),
        in_specs=[anyspec] * 5 + [smem] * 4,
        out_specs=(anyspec, anyspec, anyspec, pl.BlockSpec(memory_space=pltpu.VMEM)),
        scratch_shapes=scratch,
        compiler_params=pltpu.CompilerParams(
            collective_id=0, has_side_effects=True, vmem_limit_bytes=56 * 1024 * 1024
        ),
    )(query_rows, key_rows, value_rows, target, w_out, clip_lengths, timesteps, tile_pattern,
      tau_prev)


def solution(mesh):
    return jax.shard_map(
        on_device,
        mesh=mesh,
        in_specs=(
            P(("dp", "ctx"), None),
            P(("dp", "ctx"), None),
            P(("dp", "ctx"), None),
            P(("dp", "ctx"), None),
            P(),
            P("dp", None),
            P("dp", None),
            P("dp", None, None),
            P(),
        ),
        out_specs=(
            P(("dp", "ctx"), None),
            P(("dp", "ctx"), None),
            P(("dp", "ctx"), None),
            P("ctx", "dp"),
        ),
        check_vma=False,
    )
```

time: 210 us -> 83.3 us (0.40)
  waiting for transfers between devices: 83.3 us -> 0 us
  Pallas kernels: 0 us -> 73.1 us
  starting transfers between devices: 26 us -> 0 us
  matrix products: 25.8 us -> 0 us
  blocking collectives: 25.3 us -> 0 us
  other arithmetic: 15.5 us -> 0 us
  between operations: 16 us -> 1.29 us
  local copies, waits for them, and re-layouts: 14.7 us -> 7.61 us
    pallas_call x0 -> x1, Pallas kernels: none -> 73.1 us  [on_device(): pl.pallas_call(functools.partial(kernel, C, NY, NZ, RB, DA), out_shape=(r...]
    all_to_all x7 -> x0, waiting for transfers between devices: 39.8 us -> none  [the longest x1 7.78 us: on_device(): lax.all_to_all(query_rows, 'ctx', split_axis=1, concat_axis=0, tiled=True)]
    all_to_all x7 -> x0, starting transfers between devices: 26 us -> none  [the longest x1 4.31 us: on_device(): lax.all_to_all(jnp.concatenate(parts_v, axis=1), 'ctx', split_axis=0, con...]
    dot_general x27 -> x0, matrix products: 25.8 us -> none  [the longest x4 5.1 us: head_probs(): lax.dot_general(query_head, key_head, (((1,), (1,)), ((), ())), preferred...]
    psum x2 -> x0, blocking collectives: 25.3 us -> none  [the longest x1 19.5 us: on_device(): loss_sum = lax.psum(jnp.sum(clip_loss), 'dp')]
    reduce_scatter x1 -> x0, waiting for transfers between devices: 24.1 us -> none  [on_device(): lax.psum_scatter(block_terms.astype(jnp.bfloat16), 'dp', scatter_dimensio...]
    all_gather x1 -> x0, waiting for transfers between devices: 19.4 us -> none  [on_device(): pred_pack = lax.all_gather(pred_grad, 'ctx', axis=0, tiled=True)]
    reduce_sum x7 -> x0, other arithmetic: 6.98 us -> none  [the longest x1 2.69 us: head_probs(): row_total = jnp.sum(unnorm, axis=1)]
  transfers between devices with their start and end apart: 9 -> 0, of which waited for: 9 -> 0; matrix products, arithmetic and copies ran while one was open for 11% -> 0% of each run, Pallas kernels for 0% -> 0%
where the time goes in v1:
time: 83.3 us; the launch traced here: 82 us
  Pallas kernels  73.1 us (88%)
  local copies, waits for them, and re-layouts  7.61 us (9%)
  between operations  1.29 us (2%)
    pallas_call x1, Pallas kernels, on_device(): pl.pallas_call(functools.partial(kernel, C, NY, NZ, RB, DA), out_shape=(r...  73.1 us
    unnamed x3, local copies, waits for them, and re-layouts  5.64 us
    pallas_call x1, local copies, waits for them, and re-layouts, on_device(): pl.pallas_call(functools.partial(kernel, C, NY, NZ, RB, DA), out_shape=(r...  1.97 us

profile of v1, /device:TPU:8, one launch (start us, length us, event | category | flops | bytes accessed | tf_op | source)
XLA Modules:
  0.0 82.0 jit_solution(9333926428229800285)
XLA Ops:
  1.3 73.1 %shard_map.120 = (bf16[128,2048]{1,0:T(8,128)(2,1)}, bf16[128,2048]{1,0:T(8,128)(2,1)}, bf16[128,2048]{1,0:T(8,128)(2,1)}, f32[512,192]{1,0:T(8,128)}) custom-call(bf16[128,2048]{1,0:T(8,128)(2,1)} %q_in.1, bf16[128,2048]{1,0:T(8,128)(2,1)} %k_in.1, bf16[128,2048]{1,0:T(8,128)(2,1)} %v_in.1, bf16[128,1536]{1,0:T(8,128)(2,1)} %tgt_in.1, ...), custom_call_target="tpu_custom_call" | custom-call | tf_op jit(solution)/shard_map/pallas_call | solution.py:429
  74.4 2.0 %copy.13 = f32[512,192]{0,1:T(8,128)} copy(f32[512,192]{1,0:T(8,128)} %get-tuple-element.7) | data formatting | bytes 786432 | tf_op jit(solution)/shard_map/pallas_call | solution.py:429
  76.4 1.9 %copy.18 = bf16[128,2048]{1,0:T(8,128)(2,1)} copy(bf16[128,2048]{1,0:T(8,128)(2,1)} %get-tuple-element.12) | data formatting | bytes 1048576
  78.2 1.9 %copy.19 = bf16[128,2048]{1,0:T(8,128)(2,1)} copy(bf16[128,2048]{1,0:T(8,128)(2,1)} %get-tuple-element.13) | data formatting | bytes 1048576
  80.1 1.9 %copy.20 = bf16[128,2048]{1,0:T(8,128)(2,1)} copy(bf16[128,2048]{1,0:T(8,128)(2,1)} %get-tuple-element.14) | data formatting | bytes 1048576

commit v2 on v1

--- a/solution.py
+++ b/solution.py
@@ -184,12 +184,28 @@
         for o in range(1, C):
             out_copy(h, o).wait_recv()
 
+    def res_view(p, n):
+        return respack.at[rows(p), pl.ds(n * CHUNK, CHUNK)]
+
+    def res_copy(n, o):
+        p = sib if o == 0 else x_peer(o)
+        return remote(res_view(me, n), res_view(me, n), res_send.at[n, o], res_recv.at[n, o],
+                      {"ctx": p})
+
+    def relay_copy(n, o):
+        p = lax.rem(xi + X - o, X) * 2 + core
+        return remote(res_view(p, n), res_view(p, n), rel_send.at[n, o], rel_recv.at[n, o],
+                      {"ctx": sib})
+
     rowsq = jnp.zeros((RB, 1), F32)
     for n in range(NCH):
         cc = slice(n * CHUNK, (n + 1) * CHUNK)
         res = dot_nn(orow[...], w_v[:, cc]) - tgt_v[:, cc].astype(F32)
         rowsq = rowsq + jnp.sum(res * res, axis=1, keepdims=True)
         respack[rows(me), cc] = res.astype(BF16)
+        if n < NCH - 1:
+            for o in range(1, X):
+                res_copy(n, o).start()
 
     lane = lax.broadcasted_iota(jnp.int32, (RB, 128), 1)
     own_clip = clip_of(lax.broadcasted_iota(jnp.int32, (RB, 128), 0) + me * RB)
@@ -208,22 +224,8 @@
     for o in range(1, C):
         lctx_copy(o).start()
 
-    def res_view(p, n):
-        return respack.at[rows(p), pl.ds(n * CHUNK, CHUNK)]
-
-    def res_copy(n, o):
-        p = sib if o == 0 else x_peer(o)
-        return remote(res_view(me, n), res_view(me, n), res_send.at[n, o], res_recv.at[n, o],
-                      {"ctx": p})
-
-    def relay_copy(n, o):
-        p = lax.rem(xi + X - o, X) * 2 + core
-        return remote(res_view(p, n), res_view(p, n), rel_send.at[n, o], rel_recv.at[n, o],
-                      {"ctx": sib})
-
-    for n in range(NCH):
-        for o in range(1, X):
-            res_copy(n, o).start()
+    for o in range(1, X):
+        res_copy(NCH - 1, o).start()
     for n in range(NCH):
         res_copy(n, 0).start()
 
@@ -283,15 +285,8 @@
     for n in range(NCH):
         for o in range(1, X):
             relay_copy(n, o).wait_recv()
-    for o in range(1, X):
-        grad_rows(lax.rem(xi + X - o, X) * 2 + (1 - core))
-    for i in range(C):
-        rr = slice(i * RB, (i + 1) * RB)
-        gh[rr, :] = (graw[rr, :] * scales[i]).astype(BF16)
-
-    @pl.loop(0, OUT // 256)
-    def _(n):
-        wt[rows(n, 256), :] = dot_tn(respack[:, rows(n, 256)], osc[...]).astype(BF16)
+    def weight_rows(n, width):
+        wt[rows(n, width), :] = dot_tn(respack[:, rows(n, width)], osc[...]).astype(BF16)
 
     def wy_copy(o, k):
         kk = lax.rem(zi + k, NZ)
@@ -309,10 +304,23 @@
             total = total + yrecv[o, lax.rem(k, NZ)].astype(F32)
         return total
 
+    by_z = (NY * B) % 128 == 0
+    if not by_z:
+        pl.loop(0, OUT // 256)(lambda n: weight_rows(n, 256))
+
     @pl.loop(1, NZ + 1)
     def _(k):
+        if by_z:
+            weight_rows(lax.rem(zi + k, NZ), NY * B)
         for o in range(1, NY):
             wy_copy(o, k).start()
+
+    for o in range(1, X):
+        grad_rows(lax.rem(xi + X - o, X) * 2 + (1 - core))
+    for i in range(C):
+        rr = slice(i * RB, (i + 1) * RB)
+        gh[rr, :] = (graw[rr, :] * scales[i]).astype(BF16)
+
 
     def grad_copy(t, h, o):
         p = ctx_peer(o)
@@ -363,7 +371,7 @@
     for k in range(1, NZ):
         wz_copy(k).wait_recv()
         total = total + zrecv[k].astype(F32)
-    wg[...] = total.T
+    wg[...] = total
 
     @pl.loop(0, H)
     def _(h):
@@ -394,6 +402,23 @@
 
     for t in range(3):
         own_grad(t).wait()
+
+
+def place_kernel(*refs):
+    half = len(refs) // 2
+    sems, sources, results = refs[-1], refs[:half], refs[half:-1]
+    copies = []
+    for a, (source, result) in enumerate(zip(sources, results)):
+        pieces = 4 if source.shape[0] % 64 == 0 else 1
+        part = source.shape[0] // pieces
+        for j in range(pieces):
+            where = pl.ds(j * part, part)
+            copies.append(
+                pltpu.make_async_copy(source.at[where, :], result.at[where, :], sems.at[a, j]))
+    for copy in copies:
+        copy.start()
+    for copy in copies:
+        copy.wait()
 
 
 def on_device(
@@ -426,9 +451,10 @@
         dma((NY, NZ)), dma((NY, NZ)), dma((NZ,)), dma((NZ,)),
         dma((3, H, C)), dma((3, H, C)), dma((3,)),
     ]
-    return pl.pallas_call(
+    shapes = (rows_shape, rows_shape, rows_shape, jax.ShapeDtypeStruct((B, WD), F32))
+    results = pl.pallas_call(
         functools.partial(kernel, C, NY, NZ, RB, DA),
-        out_shape=(rows_shape, rows_shape, rows_shape, jax.ShapeDtypeStruct((WD, B), F32)),
+        out_shape=shapes,
         in_specs=[anyspec] * 5 + [smem] * 4,
         out_specs=(anyspec, anyspec, anyspec, pl.BlockSpec(memory_space=pltpu.VMEM)),
         scratch_shapes=scratch,
@@ -437,6 +463,15 @@
         ),
     )(query_rows, key_rows, value_rows, target, w_out, clip_lengths, timesteps, tile_pattern,
       tau_prev)
+    query_grad, key_grad, value_grad, weight_grad = pl.pallas_call(
+        place_kernel,
+        out_shape=shapes,
+        in_specs=[anyspec] * 4,
+        out_specs=(anyspec,) * 4,
+        scratch_shapes=[dma((4, 4))],
+        compiler_params=pltpu.CompilerParams(vmem_limit_bytes=56 * 1024 * 1024),
+    )(*results)
+    return query_grad, key_grad, value_grad, weight_grad.T
 
 
 def solution(mesh):

time: 83.3 us -> 132 us (1.58); the launches traced: 82 us -> 132 us
  Pallas kernels: 73.1 us -> 131 us
  local copies, waits for them, and re-layouts: 7.61 us -> 0 us
    pallas_call x1 -> x2, Pallas kernels: 73.1 us -> 131 us  [the longest x1 70.1 us: on_device(): pl.pallas_call(functools.partial(kernel, C, NY, NZ, RB, DA), out_shape=sh...]
    unnamed x3 -> x0, local copies, waits for them, and re-layouts: 5.64 us -> none
    pallas_call x1 -> x0, local copies, waits for them, and re-layouts: 1.97 us -> none  [on_device(): pl.pallas_call(functools.partial(kernel, C, NY, NZ, RB, DA), out_shape=(r...]
where the time goes in v2:
time: 132 us
  Pallas kernels  131 us (99%)
    pallas_call x1, Pallas kernels, on_device(): pl.pallas_call(functools.partial(kernel, C, NY, NZ, RB, DA), out_shape=sh...  70.1 us
    pallas_call x1, Pallas kernels, on_device(): pl.pallas_call(place_kernel, out_shape=shapes, in_specs=[anyspec] * 4, ou...  60.8 us

profile of v2, /device:TPU:8, one launch (start us, length us, event | category | flops | bytes accessed | tf_op | source)
XLA Modules:
  0.0 132.2 jit_solution(6254543585300939348)
XLA Ops:
  1.3 70.1 %shard_map.120 = (bf16[128,2048]{1,0:T(8,128)(2,1)}, bf16[128,2048]{1,0:T(8,128)(2,1)}, bf16[128,2048]{1,0:T(8,128)(2,1)}, f32[192,512]{1,0:T(8,128)}) custom-call(bf16[128,2048]{1,0:T(8,128)(2,1)} %q_in.1, bf16[128,2048]{1,0:T(8,128)(2,1)} %k_in.1, bf16[128,2048]{1,0:T(8,128)(2,1)} %v_in.1, bf16[128,1536]{1,0:T(8,128)(2,1)} %tgt_in.1, ...), custom_call_target="tpu_custom_call" | custom-call | tf_op jit(solution)/shard_map/pallas_call | solution.py:455
  71.4 60.8 %shard_map.121 = (bf16[128,2048]{1,0:T(8,128)(2,1)}, bf16[128,2048]{1,0:T(8,128)(2,1)}, bf16[128,2048]{1,0:T(8,128)(2,1)}, f32[192,512]{1,0:T(8,128)}) custom-call(bf16[128,2048]{1,0:T(8,128)(2,1)} %get-tuple-element.12.refs_0_, bf16[128,2048]{1,0:T(8,128)(2,1)} %get-tuple-element.13.refs_1_, bf16[128,2048]{1,0:T(8,128)(2,1)} %get-tuple-element.14.refs_2_, ...), custom_call_target="tpu_custom_call" | custom-call | tf_op jit(solution)/shard_map/pallas_call | solution.py:466

commit v3 on v2

--- a/solution.py
+++ b/solution.py
@@ -405,20 +405,26 @@
 
 
 def place_kernel(*refs):
-    half = len(refs) // 2
-    sems, sources, results = refs[-1], refs[:half], refs[half:-1]
-    copies = []
-    for a, (source, result) in enumerate(zip(sources, results)):
-        pieces = 4 if source.shape[0] % 64 == 0 else 1
-        part = source.shape[0] // pieces
+    sources, results, held = refs[:4], refs[4:8], refs[8:12]
+    in_sem, out_sem = refs[12:]
+    pairs = []
+    for a in range(4):
+        pieces = 4 if sources[a].shape[0] % 64 == 0 else 1
+        part = sources[a].shape[0] // pieces
         for j in range(pieces):
             where = pl.ds(j * part, part)
-            copies.append(
-                pltpu.make_async_copy(source.at[where, :], result.at[where, :], sems.at[a, j]))
-    for copy in copies:
-        copy.start()
-    for copy in copies:
-        copy.wait()
+            slot = held[a].at[where, :]
+            pairs.append((
+                pltpu.make_async_copy(sources[a].at[where, :], slot, in_sem.at[a, j]),
+                pltpu.make_async_copy(slot, results[a].at[where, :], out_sem.at[a, j]),
+            ))
+    for load, store in pairs:
+        load.start()
+    for load, store in pairs:
+        load.wait()
+        store.start()
+    for load, store in pairs:
+        store.wait()
 
 
 def on_device(
@@ -468,7 +474,10 @@
         out_shape=shapes,
         in_specs=[anyspec] * 4,
         out_specs=(anyspec,) * 4,
-        scratch_shapes=[dma((4, 4))],
+        scratch_shapes=[
+            vm((RB, DA), BF16), vm((RB, DA), BF16), vm((RB, DA), BF16), vm((B, WD), F32),
+            dma((4, 4)), dma((4, 4)),
+        ],
         compiler_params=pltpu.CompilerParams(vmem_limit_bytes=56 * 1024 * 1024),
     )(*results)
     return query_grad, key_grad, value_grad, weight_grad.T

time: 132 us -> 74.1 us (0.56)
  Pallas kernels: 131 us -> 72.6 us
    pallas_call x1, Pallas kernels: 60.8 us -> 2.53 us  [on_device(): pl.pallas_call(place_kernel, out_shape=shapes, in_specs=[anyspec] * 4, ou...]
where the time goes in v3:
time: 74.1 us; the launch traced here: 73.9 us
  Pallas kernels  72.6 us (98%)
  between operations  1.29 us (2%)
    pallas_call x1, Pallas kernels, on_device(): pl.pallas_call(functools.partial(kernel, C, NY, NZ, RB, DA), out_shape=sh...  70.1 us
    pallas_call x1, Pallas kernels, on_device(): pl.pallas_call(place_kernel, out_shape=shapes, in_specs=[anyspec] * 4, ou...  2.53 us

profile of v3, /device:TPU:8, one launch (start us, length us, event | category | flops | bytes accessed | tf_op | source)
XLA Modules:
  0.0 73.9 jit_solution(17751761262058125648)
XLA Ops:
  1.3 70.1 %shard_map.120 = (bf16[128,2048]{1,0:T(8,128)(2,1)}, bf16[128,2048]{1,0:T(8,128)(2,1)}, bf16[128,2048]{1,0:T(8,128)(2,1)}, f32[192,512]{1,0:T(8,128)}) custom-call(bf16[128,2048]{1,0:T(8,128)(2,1)} %q_in.1, bf16[128,2048]{1,0:T(8,128)(2,1)} %k_in.1, bf16[128,2048]{1,0:T(8,128)(2,1)} %v_in.1, bf16[128,1536]{1,0:T(8,128)(2,1)} %tgt_in.1, ...), custom_call_target="tpu_custom_call" | custom-call | tf_op jit(solution)/shard_map/pallas_call | solution.py:461
  71.4 2.5 %shard_map.121 = (bf16[128,2048]{1,0:T(8,128)(2,1)}, bf16[128,2048]{1,0:T(8,128)(2,1)}, bf16[128,2048]{1,0:T(8,128)(2,1)}, f32[192,512]{1,0:T(8,128)}) custom-call(bf16[128,2048]{1,0:T(8,128)(2,1)} %get-tuple-element.12.refs_0_, bf16[128,2048]{1,0:T(8,128)(2,1)} %get-tuple-element.13.refs_1_, bf16[128,2048]{1,0:T(8,128)(2,1)} %get-tuple-element.14.refs_2_, ...), custom_call_target="tpu_custom_call" | custom-call | tf_op jit(solution)/shard_map/pallas_call | solution.py:472

commit v4 on v3

--- a/solution.py
+++ b/solution.py
@@ -179,7 +179,24 @@
     copy_t.wait()
     copy_w.wait()
 
-    @pl.loop(0, H)
+    def partial_pred(n, low, high):
+        total = None
+        for c in range(C):
+            part_rows = slice(c * WD + low * HD, c * WD + high * HD)
+            term = dot_nn(orow[:, part_rows], w_v[part_rows, n * CHUNK:(n + 1) * CHUNK])
+            total = term if total is None else total + term
+        return total
+
+    half = max(H // 2, 1)
+
+    @pl.loop(0, half)
+    def _(h):
+        for o in range(1, C):
+            out_copy(h, o).wait_recv()
+
+    early = [partial_pred(n, 0, half) for n in range(NCH)]
+
+    @pl.loop(half, H)
     def _(h):
         for o in range(1, C):
             out_copy(h, o).wait_recv()
@@ -200,7 +217,9 @@
     rowsq = jnp.zeros((RB, 1), F32)
     for n in range(NCH):
         cc = slice(n * CHUNK, (n + 1) * CHUNK)
-        res = dot_nn(orow[...], w_v[:, cc]) - tgt_v[:, cc].astype(F32)
+        res = early[n] - tgt_v[:, cc].astype(F32)
+        if half < H:
+            res = res + partial_pred(n, half, H)
         rowsq = rowsq + jnp.sum(res * res, axis=1, keepdims=True)
         respack[rows(me), cc] = res.astype(BF16)
         if n < NCH - 1:

time: 74.1 us -> 74 us (level)
  no operation moved by 1% of the time
where the time goes in v4:
time: 74 us; the launch traced here: 73.8 us
  Pallas kernels  72.5 us (98%)
  between operations  1.29 us (2%)
    pallas_call x1, Pallas kernels, on_device(): pl.pallas_call(functools.partial(kernel, C, NY, NZ, RB, DA), out_shape=sh...  70 us
    pallas_call x1, Pallas kernels, on_device(): pl.pallas_call(place_kernel, out_shape=shapes, in_specs=[anyspec] * 4, ou...  2.53 us

profile of v4, /device:TPU:8, one launch (start us, length us, event | category | flops | bytes accessed | tf_op | source)
XLA Modules:
  0.0 73.8 jit_solution(10289741952167547205)
XLA Ops:
  1.3 70.0 %shard_map.120 = (bf16[128,2048]{1,0:T(8,128)(2,1)}, bf16[128,2048]{1,0:T(8,128)(2,1)}, bf16[128,2048]{1,0:T(8,128)(2,1)}, f32[192,512]{1,0:T(8,128)}) custom-call(bf16[128,2048]{1,0:T(8,128)(2,1)} %q_in.1, bf16[128,2048]{1,0:T(8,128)(2,1)} %k_in.1, bf16[128,2048]{1,0:T(8,128)(2,1)} %v_in.1, bf16[128,1536]{1,0:T(8,128)(2,1)} %tgt_in.1, ...), custom_call_target="tpu_custom_call" | custom-call | tf_op jit(solution)/shard_map/pallas_call | solution.py:480
  71.3 2.5 %shard_map.121 = (bf16[128,2048]{1,0:T(8,128)(2,1)}, bf16[128,2048]{1,0:T(8,128)(2,1)}, bf16[128,2048]{1,0:T(8,128)(2,1)}, f32[192,512]{1,0:T(8,128)}) custom-call(bf16[128,2048]{1,0:T(8,128)(2,1)} %get-tuple-element.12.refs_0_, bf16[128,2048]{1,0:T(8,128)(2,1)} %get-tuple-element.13.refs_1_, bf16[128,2048]{1,0:T(8,128)(2,1)} %get-tuple-element.14.refs_2_, ...), custom_call_target="tpu_custom_call" | custom-call | tf_op jit(solution)/shard_map/pallas_call | solution.py:491
